TPU v7x, 32 devices: a whole 2x2x4 slice. The times are simulated.
32 devices in a mesh: row: 8 (over z, y), col: 4 (over x, core).
Axes of the slice: x: 2, y: 2, z: 4, core: 2. Of those that a mesh axis runs over, the one named last changes fastest.
Arguments:
- noise: float32 [2, 3072, 512], P(None, 'row', 'col'), may hold values from -6 to 6
- kappa: float32 [3072, 512], P('row', 'col'), may hold values from 0.2 to 1
- metric: float32 [3072, 512], P('row', 'col'), may hold values from 0.3 to 1
- edge_src: int32 [24], replicated, may hold values from 0 to 23, each once
- edge_rev: int32 [24], replicated, may hold values from 0 to 1
- corner_src: int32 [24], replicated, may hold values from 0 to 47
Outputs:
- sample: float32 [2, 3072, 512], P(None, 'row', 'col')
Inputs may be any that keep to these rules, and one draw needn't show every extreme that they name: `edge_src`: every line number appears once.
All inputs are finite; a program needn't handle non-finite values.
Results may differ from a plain program's by a relative error of at most 0.00011.
Values sent between devices are 32-bit elements; how exact they have to be, the bound alone decides.
A program may use at most 64 MiB of HBM per device.

v0:
```python
import functools
import math

import jax
import jax.numpy as jnp
from jax import lax
from jax.experimental import pallas as pl
from jax.experimental.pallas import tpu as pltpu
from jax.sharding import PartitionSpec as P

SWEEPS = 4
LANES = 128
MESH = pl.DeviceIdType.MESH


def kernel(
    dims, noise, kappa, metric, esrc, erev, csrc, out,
    field, rate, area, hsum, picked, flags, cols, *rest
):
    levels, rows, width, nr, nc = dims
    packs, stages, halos = rest[0:4], rest[4:8], rest[8:12]
    in_sem, pack_send, pack_recv, halo_send, halo_recv = rest[12:17]
    ndev = nr * nc
    face = width * nc
    total = 6 * face
    offset = face // 2
    unit = math.gcd(math.gcd(rows, offset), width)
    nu = rows // unit
    nw = width // unit
    per_face = face // unit
    short, full = 2 * nw, 2 * nw + nu

    i = lax.axis_index("row")
    c = lax.axis_index("col")
    me = i * nc + c
    left = c == 0
    right = c == nc - 1
    side = jnp.logical_or(left, right)

    loads = [
        pltpu.make_async_copy(noise, field, in_sem.at[0]),
        pltpu.make_async_copy(kappa, rate, in_sem.at[1]),
        pltpu.make_async_copy(metric, area, in_sem.at[2]),
    ]
    for load in loads:
        load.start()

    barrier = pltpu.get_barrier_semaphore()

    def greet(k, carry):
        d = lax.rem(me + k, ndev)
        pl.semaphore_signal(
            barrier, inc=1, device_id=(lax.div(d, nc), lax.rem(d, nc)), device_id_type=MESH
        )
        return carry

    lax.fori_loop(1, ndev, greet, 0)

    start = lax.rem(i * rows + offset, total)
    f0 = lax.div(start, face)
    into = start - f0 * face
    has_top = jnp.logical_or(into == 0, into + rows > face)
    has_bottom = into + rows >= face
    top_face = jnp.where(into == 0, f0, lax.rem(f0 + 1, 6))
    top_row = jnp.where(into == 0, 0, face - into)
    bottom_row = face - 1 - into
    top_at = jnp.where(has_top, top_row, 0)
    bottom_at = jnp.where(has_bottom, bottom_row, 0)
    top_hit = jnp.where(has_top, top_row, -1)
    bottom_hit = jnp.where(has_bottom, bottom_row, -1)

    def place(line, u):
        f = lax.div(line, 4)
        e = lax.rem(line, 4)
        row_stored = lax.rem(f * face + jnp.where(e == 1, face - 1, 0) + total - offset, total)
        row_at = (lax.div(row_stored, rows) * nc + lax.div(u, nw)) * full + e * nw + lax.rem(u, nw)
        side_stored = lax.rem(f * face + u * unit + total - offset, total)
        d = lax.div(side_stored, rows)
        k = lax.div(side_stored - d * rows, unit)
        side_at = (d * nc + jnp.where(e == 3, nc - 1, 0)) * full + short + k
        return jnp.where(e < 2, row_at, side_at)

    def ghost_unit(edge, u):
        turned = erev[edge]
        return place(esrc[edge], jnp.where(turned == 1, per_face - 1 - u, u)), turned

    def corner(index):
        s = csrc[index]
        end = lax.rem(s, 2)
        return place(lax.div(s, 2), end * (per_face - 1)), end

    def ghost_cell(edge, u, end):
        turned = erev[edge]
        at = place(esrc[edge], jnp.where(turned == 1, per_face - 1 - u, u))
        return at, jnp.where(turned == 1, 1 - end, end)

    def choose(flag, a, b):
        return jnp.where(flag, a[0], b[0]), jnp.where(flag, a[1], b[1])

    items = []
    bottom_face = f0
    for f, e, q0 in ((top_face, 0, 0), (bottom_face, 1, 2)):
        edge = 4 * f + e
        for k in range(nw):
            items.append(ghost_unit(edge, c * nw + k))
        before = ghost_cell(edge, jnp.maximum(c * nw - 1, 0), 1)
        after = ghost_cell(edge, jnp.minimum(c * nw + nw, per_face - 1), 0)
        items.append(choose(left, corner(4 * f + q0), before))
        items.append(choose(right, corner(4 * f + q0 + 1), after))
    side_edge = jnp.where(left, 2, 3)
    for k in range(nu):
        at = lax.rem(start + k * unit, total)
        f = lax.div(at, face)
        items.append(ghost_unit(4 * f + side_edge, lax.div(at - f * face, unit)))
    at = lax.rem(start + total - unit, total)
    f = lax.div(at, face)
    items.append(ghost_cell(4 * f + side_edge, lax.div(at - f * face, unit), 1))
    at = lax.rem(start + rows, total)
    f = lax.div(at, face)
    items.append(ghost_cell(4 * f + side_edge, lax.div(at - f * face, unit), 0))
    top0, bottom0, side0 = 0, nw + 2, 2 * (nw + 2)
    up_cell, down_cell = side0 + nu, side0 + nu + 1
    for n, (_, flip) in enumerate(items):
        flags[n * levels : (n + 1) * levels, :] = jnp.full((levels, LANES), flip, jnp.int32)

    lane = lax.broadcasted_iota(jnp.int32, (unit, LANES), 1)
    local_row = lax.broadcasted_iota(jnp.int32, (unit, LANES), 0)
    small_lane = lax.broadcasted_iota(jnp.int32, (8, LANES), 1)
    turn = lax.rem(
        unit - 1 - lax.broadcasted_iota(jnp.int32, (picked.shape[0], LANES), 1) + LANES, LANES
    )

    base = me * full
    up = lax.rem(i + nr - 1, nr)
    down = lax.rem(i + 1, nr)
    west = lax.rem(c + nc - 1, nc)
    east = lax.rem(c + 1, nc)

    def prepare(s):
        pack, stage = packs[s], stages[s]
        for l in range(levels):
            stage[0, l : l + 1, :] = field[l, 0:1, :]
            stage[1, l : l + 1, :] = field[l, rows - 1 : rows, :]
            for e, row in ((0, top_at), (1, bottom_at)):
                line = field[l, pl.ds(row, 1), :]
                for k in range(nw):
                    part = line if k == 0 else jnp.roll(line, -k * unit, axis=1)
                    pack[base + e * nw + k, l : l + 1, :] = part
        for k in range(nu):
            both = jnp.zeros((unit, LANES), jnp.float32)
            for l in range(levels):
                block = field[l, k * unit : (k + 1) * unit, :]
                both = jnp.where(lane >= 2 * l, pltpu.roll(block, 1 + 2 * l, 1), both)
            turned = both.T
            for l in range(levels):
                last = turned[2 * l : 2 * l + 1, :]
                first = turned[2 * l + 1 : 2 * l + 2, :]
                stage[2 + k, l : l + 1, 0:unit] = first
                stage[2 + nu + k, l : l + 1, 0:unit] = last
                pack[base + short + k, l : l + 1, 0:unit] = jnp.where(left, first, last)

    def send(s):
        pack, stage, halo = packs[s], stages[s], halos[s]

        def near(src, dst, size, where):
            pltpu.make_async_remote_copy(
                stage.at[pl.ds(src, size)], halo.at[pl.ds(dst, size)],
                halo_send.at[s], halo_recv.at[s], device_id=where, device_id_type=MESH,
            ).start()

        def far(size):
            def step(k, carry):
                d = lax.rem(me + k, ndev)
                mine = pack.at[pl.ds(base, size)]
                pltpu.make_async_remote_copy(
                    mine, mine, pack_send.at[s], pack_recv.at[s],
                    device_id=(lax.div(d, nc), lax.rem(d, nc)), device_id_type=MESH,
                ).start()
                return carry

            lax.fori_loop(1, ndev, step, 0)

        @pl.when(side)
        def _():
            far(full)

        @pl.when(jnp.logical_not(side))
        def _():
            far(short)

        near(0, 1, 1, (up, c))
        near(0, 5, 1, (up, west))
        near(0, 4, 1, (up, east))
        near(1, 0, 1, (down, c))
        near(1, 3, 1, (down, west))
        near(1, 2, 1, (down, east))
        near(2, 6 + nu, nu, (i, west))
        near(2 + nu, 6, nu, (i, east))

    everything = 2 * nr * full + (nc - 2) * nr * short

    def pack_wait(s, sem, side_units, mid_units):
        pack = packs[s]

        def take(units):
            part = pack.at[pl.ds(0, units)]
            pltpu.make_async_copy(part, part, sem.at[s]).wait()

        @pl.when(side)
        def _():
            take(side_units)

        @pl.when(jnp.logical_not(side))
        def _():
            take(mid_units)

    def receive(s):
        halo = halos[s]
        pltpu.make_async_copy(halo, halo, halo_recv.at[s]).wait()
        pack_wait(s, pack_recv, everything - full, everything - short)

    def finish(s):
        halo = halos[s]
        pltpu.make_async_copy(halo, halo, halo_send.at[s]).wait()
        pack_wait(s, pack_send, (ndev - 1) * full, (ndev - 1) * short)

    def triple(mid, before, after):
        mid, before, after = (
            jnp.concatenate([x, jnp.zeros((8 - x.shape[0], LANES), jnp.float32)], axis=0)
            for x in (mid, before, after)
        )
        west_of = jnp.where(small_lane == 0, before, pltpu.roll(mid, 1, 1))
        east_of = jnp.where(
            small_lane == LANES - 1, pltpu.roll(after, LANES - 1, 1), pltpu.roll(mid, LANES - 1, 1)
        )
        return mid + west_of + east_of

    def sweep(s, dest):
        pack, halo = packs[s], halos[s]
        for n, (at, _) in enumerate(items):
            picked[n * levels : (n + 1) * levels, :] = pack[at]
        raw = picked[...]
        picked[...] = jnp.where(flags[...] == 1, jnp.take_along_axis(raw, turn, axis=1), raw)

        def item(n):
            return picked[n * levels : (n + 1) * levels, :]

        def whole_line(n):
            if nw == 1:
                return item(n)
            return jnp.concatenate([item(n + k)[:, 0:unit] for k in range(nw)], axis=1)

        for k in range(nu):
            own = item(side0 + k)
            at = k * 2 * levels
            cols[at : at + levels, :] = jnp.where(left, own, halo[6 + k])
            cols[at + levels : at + 2 * levels, :] = jnp.where(right, own, halo[6 + nu + k])
        columns = cols[...].T

        ghost_top = triple(whole_line(top0), item(top0 + nw), item(top0 + nw + 1))
        ghost_bottom = triple(whole_line(bottom0), item(bottom0 + nw), item(bottom0 + nw + 1))

        def end_of(x):
            return jnp.concatenate([x[:, LANES - 1 :], x[:, : LANES - 1]], axis=1)

        above = triple(
            halo[0],
            jnp.where(left, item(up_cell), end_of(halo[2])),
            jnp.where(right, item(up_cell), halo[3]),
        )
        below = triple(
            halo[1],
            jnp.where(left, item(down_cell), end_of(halo[4])),
            jnp.where(right, item(down_cell), halo[5]),
        )
        for l in range(levels):
            hsum[l, 7:8, :] = above[l : l + 1]
            hsum[l, 8 + rows : 9 + rows, :] = below[l : l + 1]
            for k in range(nu):
                x = field[l, k * unit : (k + 1) * unit, :]
                j = k * 2 * levels + l
                w = columns[0:unit, j : j + 1]
                e = columns[0:unit, j + levels : j + levels + 1]
                west_of = jnp.where(lane == 0, w, pltpu.roll(x, 1, 1))
                east_of = jnp.where(lane == LANES - 1, e, pltpu.roll(x, LANES - 1, 1))
                hsum[l, 8 + k * unit : 8 + (k + 1) * unit, :] = x + west_of + east_of
        for l in range(levels):
            for k in range(nu):
                r0 = k * unit
                x = field[l, r0 : r0 + unit, :]
                upper = jnp.where(
                    local_row == top_hit - r0, ghost_top[l : l + 1], hsum[l, 7 + r0 : 7 + r0 + unit, :]
                )
                lower = jnp.where(
                    local_row == bottom_hit - r0,
                    ghost_bottom[l : l + 1],
                    hsum[l, 9 + r0 : 9 + r0 + unit, :],
                )
                box = upper + hsum[l, 8 + r0 : 8 + r0 + unit, :] + lower
                dest[l, r0 : r0 + unit, :] = x + rate[r0 : r0 + unit, :] * (box - 9.0 * x)

    loads[0].wait()
    prepare(0)
    loads[1].wait()
    loads[2].wait()
    rate[...] = rate[...] * area[...] * 0.125
    pl.semaphore_wait(barrier, ndev - 1)
    for s in range(SWEEPS):
        send(s)
        receive(s)
        sweep(s, out if s == SWEEPS - 1 else field)
        if s < SWEEPS - 1:
            prepare(s + 1)
    for s in range(SWEEPS):
        finish(s)


def on_device(noise, kappa, metric, edge_src, edge_rev, corner_src):
    levels, rows, width = noise.shape
    nr, nc = lax.axis_size("row"), lax.axis_size("col")
    unit = math.gcd(math.gcd(rows, width * nc // 2), width)
    nu, nw = rows // unit, width // unit
    count = 2 * (nw + 2) + nu + 2
    picked_rows = -(-count * levels // 8) * 8
    col_rows = -(-nu * 2 * levels // 8) * 8
    full = 2 * nw + nu
    scratch = [
        pltpu.VMEM((levels, rows, width), jnp.float32),
        pltpu.VMEM((rows, width), jnp.float32),
        pltpu.VMEM((rows, width), jnp.float32),
        pltpu.VMEM((levels, rows + 16, width), jnp.float32),
        pltpu.VMEM((picked_rows, LANES), jnp.float32),
        pltpu.VMEM((picked_rows, LANES), jnp.int32),
        pltpu.VMEM((col_rows, LANES), jnp.float32),
    ]
    scratch += [pltpu.VMEM((nr * nc * full, levels, LANES), jnp.float32)] * SWEEPS
    scratch += [pltpu.VMEM((2 + 2 * nu, levels, LANES), jnp.float32)] * SWEEPS
    scratch += [pltpu.VMEM((6 + 2 * nu, levels, LANES), jnp.float32)] * SWEEPS
    scratch += [pltpu.SemaphoreType.DMA((3,))]
    scratch += [pltpu.SemaphoreType.DMA((SWEEPS,))] * 4
    anywhere = pl.BlockSpec(memory_space=pl.ANY)
    small = pl.BlockSpec(memory_space=pltpu.SMEM)
    return pl.pallas_call(
        functools.partial(kernel, (levels, rows, width, nr, nc)),
        out_shape=jax.ShapeDtypeStruct(noise.shape, jnp.float32),
        in_specs=[anywhere] * 3 + [small] * 3,
        out_specs=pl.BlockSpec(memory_space=pltpu.VMEM),
        scratch_shapes=scratch,
        compiler_params=pltpu.CompilerParams(
            collective_id=0, has_side_effects=True, vmem_limit_bytes=48 * 1024 * 1024
        ),
    )(noise, kappa, metric, edge_src, edge_rev, corner_src)


def solution(mesh):
    in_specs = (P(None, "row", "col"), P("row", "col"), P("row", "col"), P(), P(), P())
    out_specs = P(None, "row", "col")
    return jax.shard_map(
        on_device, mesh=mesh, in_specs=in_specs, out_specs=out_specs, check_vma=False
    )
```

profile of v0, /device:TPU:0, one launch (start us, length us, event | category | flops | bytes accessed | tf_op | source)
XLA Modules:
  0.0 40.2 jit_solution(711025818112058880)
XLA Ops:
  0.0 0.0 copy-start
  0.0 1.0 %copy-done = f32[2,384,128]{2,1,0:T(8,128)S(1)} copy-done((f32[2,384,128]{2,1,0:T(8,128)S(1)}, f32[2,384,128]{2,1,0:T(8,128)}, u32[]{:S(2)}) %copy-start) | copy-done | bytes 393240
  1.0 0.0 copy-start.1
  1.0 0.9 %copy-done.1 = f32[384,128]{1,0:T(8,128)S(1)} copy-done((f32[384,128]{1,0:T(8,128)S(1)}, f32[384,128]{1,0:T(8,128)}, u32[]{:S(2)}) %copy-start.1) | copy-done | bytes 196632
  1.9 0.0 copy-start.2
  1.9 0.9 %copy-done.2 = f32[384,128]{1,0:T(8,128)S(1)} copy-done((f32[384,128]{1,0:T(8,128)S(1)}, f32[384,128]{1,0:T(8,128)}, u32[]{:S(2)}) %copy-start.2) | copy-done | bytes 196632
  2.9 0.0 copy-start.3
  2.9 0.7 %copy-done.3 = s32[24]{0:T(128)S(1)} copy-done((s32[24]{0:T(128)S(1)}, s32[24]{0:T(128)}, u32[]{:S(2)}) %copy-start.3) | copy-done | bytes 120
  3.5 0.0 copy-start.4
  3.5 0.7 %copy-done.4 = s32[24]{0:T(128)S(1)} copy-done((s32[24]{0:T(128)S(1)}, s32[24]{0:T(128)}, u32[]{:S(2)}) %copy-start.4) | copy-done | bytes 120
  4.2 0.0 copy-start.5
  4.2 0.7 %copy-done.5 = s32[24]{0:T(128)S(1)} copy-done((s32[24]{0:T(128)S(1)}, s32[24]{0:T(128)}, u32[]{:S(2)}) %copy-start.5) | copy-done | bytes 120
  4.8 34.6 %shard_map.64 = f32[2,384,128]{2,1,0:T(8,128)S(1)} custom-call(f32[2,384,128]{2,1,0:T(8,128)S(1)} %copy-done, f32[384,128]{1,0:T(8,128)S(1)} %copy-done.1, f32[384,128]{1,0:T(8,128)S(1)} %copy-done.2, s32[24]{0:T(128)S(1)} %copy-done.3, s32[24]{0:T(128)S(1)} %copy-done.4, s32[24]{0:T(128)S(1)} %copy-done.5), custom_call_target="tpu_custom_call" | custom-call | tf_op jit(solution)/shard_map/pallas_call | solution.py:343
  39.5 0.7 %copy.8 = f32[2,384,128]{2,1,0:T(8,128)} copy(f32[2,384,128]{2,1,0:T(8,128)S(1)} %shard_map.64) | data formatting | bytes 786432
Async XLA Ops:
  0.0 1.0 %copy-start = (f32[2,384,128]{2,1,0:T(8,128)S(1)}, f32[2,384,128]{2,1,0:T(8,128)}, u32[]{:S(2)}) copy-start(f32[2,384,128]{2,1,0:T(8,128)} %noise.1) | copy-start | bytes 1179652
  1.0 0.9 %copy-start.1 = (f32[384,128]{1,0:T(8,128)S(1)}, f32[384,128]{1,0:T(8,128)}, u32[]{:S(2)}) copy-start(f32[384,128]{1,0:T(8,128)} %kappa.1) | copy-start | bytes 589828
  1.9 0.9 %copy-start.2 = (f32[384,128]{1,0:T(8,128)S(1)}, f32[384,128]{1,0:T(8,128)}, u32[]{:S(2)}) copy-start(f32[384,128]{1,0:T(8,128)} %metric.1) | copy-start | bytes 589828
  2.9 0.7 %copy-start.3 = (s32[24]{0:T(128)S(1)}, s32[24]{0:T(128)}, u32[]{:S(2)}) copy-start(s32[24]{0:T(128)} %esrc.1) | copy-start | bytes 292
  3.5 0.7 %copy-start.4 = (s32[24]{0:T(128)S(1)}, s32[24]{0:T(128)}, u32[]{:S(2)}) copy-start(s32[24]{0:T(128)} %erev.1) | copy-start | bytes 292
  4.2 0.7 %copy-start.5 = (s32[24]{0:T(128)S(1)}, s32[24]{0:T(128)}, u32[]{:S(2)}) copy-start(s32[24]{0:T(128)} %csrc.1) | copy-start | bytes 292
where the time goes:
time: 40.4 us; the launch traced here: 40.2 us
  Pallas kernels  34.6 us (86%)
  local copies, waits for them, and re-layouts  5.56 us (14%)
    pallas_call x1, Pallas kernels, on_device(): pl.pallas_call(functools.partial(kernel, (levels, rows, width, nr, nc)),...  34.6 us
    unnamed x13, local copies, waits for them, and re-layouts  5.56 us

commit v1 on v0

--- a/solution.py
+++ b/solution.py
@@ -14,12 +14,12 @@
 
 
 def kernel(
-    dims, noise, kappa, metric, esrc, erev, csrc, out,
+    dims, noise, kappa, metric, esrc_in, erev_in, csrc_in, out,
     field, rate, area, hsum, picked, flags, cols, *rest
 ):
     levels, rows, width, nr, nc = dims
     packs, stages, halos = rest[0:4], rest[4:8], rest[8:12]
-    in_sem, pack_send, pack_recv, halo_send, halo_recv = rest[12:17]
+    in_sem, pack_send, pack_recv, halo_send, halo_recv, esrc, erev, csrc = rest[12:20]
     ndev = nr * nc
     face = width * nc
     total = 6 * face
@@ -41,6 +41,9 @@
         pltpu.make_async_copy(noise, field, in_sem.at[0]),
         pltpu.make_async_copy(kappa, rate, in_sem.at[1]),
         pltpu.make_async_copy(metric, area, in_sem.at[2]),
+        pltpu.make_async_copy(esrc_in, esrc, in_sem.at[3]),
+        pltpu.make_async_copy(erev_in, erev, in_sem.at[4]),
+        pltpu.make_async_copy(csrc_in, csrc, in_sem.at[5]),
     ]
     for load in loads:
         load.start()
@@ -55,6 +58,9 @@
         return carry
 
     lax.fori_loop(1, ndev, greet, 0)
+
+    for load in loads[3:]:
+        load.wait()
 
     start = lax.rem(i * rows + offset, total)
     f0 = lax.div(start, face)
@@ -180,14 +186,6 @@
 
             lax.fori_loop(1, ndev, step, 0)
 
-        @pl.when(side)
-        def _():
-            far(full)
-
-        @pl.when(jnp.logical_not(side))
-        def _():
-            far(short)
-
         near(0, 1, 1, (up, c))
         near(0, 5, 1, (up, west))
         near(0, 4, 1, (up, east))
@@ -196,6 +194,14 @@
         near(1, 2, 1, (down, east))
         near(2, 6 + nu, nu, (i, west))
         near(2 + nu, 6, nu, (i, east))
+
+        @pl.when(side)
+        def _():
+            far(full)
+
+        @pl.when(jnp.logical_not(side))
+        def _():
+            far(short)
 
     everything = 2 * nr * full + (nc - 2) * nr * short
 
@@ -336,14 +342,14 @@
     scratch += [pltpu.VMEM((nr * nc * full, levels, LANES), jnp.float32)] * SWEEPS
     scratch += [pltpu.VMEM((2 + 2 * nu, levels, LANES), jnp.float32)] * SWEEPS
     scratch += [pltpu.VMEM((6 + 2 * nu, levels, LANES), jnp.float32)] * SWEEPS
-    scratch += [pltpu.SemaphoreType.DMA((3,))]
+    scratch += [pltpu.SemaphoreType.DMA((6,))]
     scratch += [pltpu.SemaphoreType.DMA((SWEEPS,))] * 4
-    anywhere = pl.BlockSpec(memory_space=pl.ANY)
-    small = pl.BlockSpec(memory_space=pltpu.SMEM)
+    scratch += [pltpu.SMEM(edge_src.shape, jnp.int32)] * 3
+    in_hbm = pl.BlockSpec(memory_space=pltpu.HBM)
     return pl.pallas_call(
         functools.partial(kernel, (levels, rows, width, nr, nc)),
         out_shape=jax.ShapeDtypeStruct(noise.shape, jnp.float32),
-        in_specs=[anywhere] * 3 + [small] * 3,
+        in_specs=[in_hbm] * 6,
         out_specs=pl.BlockSpec(memory_space=pltpu.VMEM),
         scratch_shapes=scratch,
         compiler_params=pltpu.CompilerParams(

time: 40.4 us -> 37.7 us (0.933)
  Pallas kernels: 34.6 us -> 31.9 us
    pallas_call x1, Pallas kernels: 34.6 us -> 31.9 us  [on_device(): pl.pallas_call(functools.partial(kernel, (levels, rows, width, nr, nc)),...]
where the time goes in v1:
time: 37.7 us; the launch traced here: 37.5 us
  Pallas kernels  31.9 us (85%)
  local copies, waits for them, and re-layouts  5.56 us (15%)
    pallas_call x1, Pallas kernels, on_device(): pl.pallas_call(functools.partial(kernel, (levels, rows, width, nr, nc)),...  31.9 us
    unnamed x13, local copies, waits for them, and re-layouts  5.56 us

profile of v1, /device:TPU:0, one launch (start us, length us, event | category | flops | bytes accessed | tf_op | source)
XLA Modules:
  0.0 37.5 jit_solution(7796498207317445084)
XLA Ops:
  0.0 0.0 copy-start
  0.0 1.0 %copy-done = f32[2,384,128]{2,1,0:T(8,128)S(1)} copy-done((f32[2,384,128]{2,1,0:T(8,128)S(1)}, f32[2,384,128]{2,1,0:T(8,128)}, u32[]{:S(2)}) %copy-start) | copy-done | bytes 393240
  1.0 0.0 copy-start.1
  1.0 0.9 %copy-done.1 = f32[384,128]{1,0:T(8,128)S(1)} copy-done((f32[384,128]{1,0:T(8,128)S(1)}, f32[384,128]{1,0:T(8,128)}, u32[]{:S(2)}) %copy-start.1) | copy-done | bytes 196632
  1.9 0.0 copy-start.2
  1.9 0.9 %copy-done.2 = f32[384,128]{1,0:T(8,128)S(1)} copy-done((f32[384,128]{1,0:T(8,128)S(1)}, f32[384,128]{1,0:T(8,128)}, u32[]{:S(2)}) %copy-start.2) | copy-done | bytes 196632
  2.9 0.0 copy-start.3
  2.9 0.7 %copy-done.3 = s32[24]{0:T(128)S(1)} copy-done((s32[24]{0:T(128)S(1)}, s32[24]{0:T(128)}, u32[]{:S(2)}) %copy-start.3) | copy-done | bytes 120
  3.5 0.0 copy-start.4
  3.5 0.7 %copy-done.4 = s32[24]{0:T(128)S(1)} copy-done((s32[24]{0:T(128)S(1)}, s32[24]{0:T(128)}, u32[]{:S(2)}) %copy-start.4) | copy-done | bytes 120
  4.2 0.0 copy-start.5
  4.2 0.7 %copy-done.5 = s32[24]{0:T(128)S(1)} copy-done((s32[24]{0:T(128)S(1)}, s32[24]{0:T(128)}, u32[]{:S(2)}) %copy-start.5) | copy-done | bytes 120
  4.8 31.9 %shard_map.64 = f32[2,384,128]{2,1,0:T(8,128)S(1)} custom-call(f32[2,384,128]{2,1,0:T(8,128)S(1)} %copy-done, f32[384,128]{1,0:T(8,128)S(1)} %copy-done.1, f32[384,128]{1,0:T(8,128)S(1)} %copy-done.2, s32[24]{0:T(128)S(1)} %copy-done.3, s32[24]{0:T(128)S(1)} %copy-done.4, s32[24]{0:T(128)S(1)} %copy-done.5), custom_call_target="tpu_custom_call" | custom-call | tf_op jit(solution)/shard_map/pallas_call | solution.py:349
  36.7 0.7 %copy.8 = f32[2,384,128]{2,1,0:T(8,128)} copy(f32[2,384,128]{2,1,0:T(8,128)S(1)} %shard_map.64) | data formatting | bytes 786432
Async XLA Ops:
  0.0 1.0 %copy-start = (f32[2,384,128]{2,1,0:T(8,128)S(1)}, f32[2,384,128]{2,1,0:T(8,128)}, u32[]{:S(2)}) copy-start(f32[2,384,128]{2,1,0:T(8,128)} %noise.1) | copy-start | bytes 1179652
  1.0 0.9 %copy-start.1 = (f32[384,128]{1,0:T(8,128)S(1)}, f32[384,128]{1,0:T(8,128)}, u32[]{:S(2)}) copy-start(f32[384,128]{1,0:T(8,128)} %kappa.1) | copy-start | bytes 589828
  1.9 0.9 %copy-start.2 = (f32[384,128]{1,0:T(8,128)S(1)}, f32[384,128]{1,0:T(8,128)}, u32[]{:S(2)}) copy-start(f32[384,128]{1,0:T(8,128)} %metric.1) | copy-start | bytes 589828
  2.9 0.7 %copy-start.3 = (s32[24]{0:T(128)S(1)}, s32[24]{0:T(128)}, u32[]{:S(2)}) copy-start(s32[24]{0:T(128)} %esrc_in.1) | copy-start | bytes 292
  3.5 0.7 %copy-start.4 = (s32[24]{0:T(128)S(1)}, s32[24]{0:T(128)}, u32[]{:S(2)}) copy-start(s32[24]{0:T(128)} %erev_in.1) | copy-start | bytes 292
  4.2 0.7 %copy-start.5 = (s32[24]{0:T(128)S(1)}, s32[24]{0:T(128)}, u32[]{:S(2)}) copy-start(s32[24]{0:T(128)} %csrc_in.1) | copy-start | bytes 292

commit v2 on v1

--- a/solution.py
+++ b/solution.py
@@ -15,7 +15,7 @@
 
 def kernel(
     dims, noise, kappa, metric, esrc_in, erev_in, csrc_in, out,
-    field, rate, area, hsum, picked, flags, cols, *rest
+    field, other, rate, area, hsum, picked, flags, *rest
 ):
     levels, rows, width, nr, nc = dims
     packs, stages, halos = rest[0:4], rest[4:8], rest[8:12]
@@ -136,13 +136,23 @@
         unit - 1 - lax.broadcasted_iota(jnp.int32, (picked.shape[0], LANES), 1) + LANES, LANES
     )
 
+    wide = (8, levels * LANES)
+    goal = lax.broadcasted_iota(jnp.int32, wide, 1)
+    source = lax.broadcasted_iota(jnp.int32, wide, 0)
+    spread = jnp.zeros(wide, jnp.float32)
+    for l in range(levels):
+        spread = jnp.where(jnp.logical_and(source == l, goal == l * LANES), 1.0, spread)
+        spread = jnp.where(
+            jnp.logical_and(source == levels + l, goal == (l + 1) * LANES - 1), 1.0, spread
+        )
+
     base = me * full
     up = lax.rem(i + nr - 1, nr)
     down = lax.rem(i + 1, nr)
     west = lax.rem(c + nc - 1, nc)
     east = lax.rem(c + 1, nc)
 
-    def prepare(s):
+    def prepare(s, field):
         pack, stage = packs[s], stages[s]
         for l in range(levels):
             stage[0, l : l + 1, :] = field[l, 0:1, :]
@@ -241,7 +251,27 @@
         )
         return mid + west_of + east_of
 
-    def sweep(s, dest):
+    def partial(src, dest):
+        for l in range(levels):
+            for k in range(nu):
+                x = src[l, k * unit : (k + 1) * unit, :]
+                west_of = jnp.where(lane == 0, 0.0, pltpu.roll(x, 1, 1))
+                east_of = jnp.where(lane == LANES - 1, 0.0, pltpu.roll(x, LANES - 1, 1))
+                hsum[l, 8 + k * unit : 8 + (k + 1) * unit, :] = x + west_of + east_of
+        for l in range(levels):
+            for k in range(nu):
+                r0 = k * unit
+                x = src[l, r0 : r0 + unit, :]
+                upper = jnp.where(
+                    local_row == top_hit - r0, 0.0, hsum[l, 7 + r0 : 7 + r0 + unit, :]
+                )
+                lower = jnp.where(
+                    local_row == bottom_hit - r0, 0.0, hsum[l, 9 + r0 : 9 + r0 + unit, :]
+                )
+                box = upper + hsum[l, 8 + r0 : 8 + r0 + unit, :] + lower
+                dest[l, r0 : r0 + unit, :] = x + rate[r0 : r0 + unit, :] * (box - 9.0 * x)
+
+    def gather(s):
         pack, halo = packs[s], halos[s]
         for n, (at, _) in enumerate(items):
             picked[n * levels : (n + 1) * levels, :] = pack[at]
@@ -256,12 +286,34 @@
                 return item(n)
             return jnp.concatenate([item(n + k)[:, 0:unit] for k in range(nw)], axis=1)
 
+        sides = []
+        blank = jnp.zeros((8 - 2 * levels, LANES), jnp.float32)
         for k in range(nu):
             own = item(side0 + k)
-            at = k * 2 * levels
-            cols[at : at + levels, :] = jnp.where(left, own, halo[6 + k])
-            cols[at + levels : at + 2 * levels, :] = jnp.where(right, own, halo[6 + nu + k])
-        columns = cols[...].T
+            w = jnp.where(left, own, halo[6 + k])
+            e = jnp.where(right, own, halo[6 + nu + k])
+            both = jnp.concatenate([w, e, blank], axis=0)
+            sides.append(both if unit == LANES else jnp.where(small_lane < unit, both, 0.0))
+        nothing = jnp.zeros((8, LANES), jnp.float32)
+        beside = []
+        for k in range(nu):
+            r0 = k * unit
+            before = sides[k - 1] if k else nothing
+            after = sides[k + 1] if k < nu - 1 else nothing
+            prev = jnp.where(
+                small_lane == 0,
+                pltpu.roll(before, (LANES + 1 - unit) % LANES, 1),
+                pltpu.roll(sides[k], 1, 1),
+            )
+            follow = jnp.where(
+                small_lane == unit - 1,
+                pltpu.roll(after, unit - 1, 1),
+                pltpu.roll(sides[k], LANES - 1, 1),
+            )
+            prev = jnp.where(small_lane == top_hit - r0, 0.0, prev)
+            follow = jnp.where(small_lane == bottom_hit - r0, 0.0, follow)
+            sums = sides[k] + prev + follow
+            beside.append(sums if unit == LANES else jnp.where(small_lane < unit, sums, 0.0))
 
         ghost_top = triple(whole_line(top0), item(top0 + nw), item(top0 + nw + 1))
         ghost_bottom = triple(whole_line(bottom0), item(bottom0 + nw), item(bottom0 + nw + 1))
@@ -279,44 +331,116 @@
             jnp.where(left, item(down_cell), end_of(halo[4])),
             jnp.where(right, item(down_cell), halo[5]),
         )
-        for l in range(levels):
-            hsum[l, 7:8, :] = above[l : l + 1]
-            hsum[l, 8 + rows : 9 + rows, :] = below[l : l + 1]
+        return beside, (
+            (0, top_hit != 0, above),
+            (rows - 1, bottom_hit != rows - 1, below),
+            (top_at, has_top, ghost_top),
+            (bottom_at, has_bottom, ghost_bottom),
+        )
+
+    def complete(dest, found):
+        beside, lines = found
+        for k in range(nu):
+            r0 = k * unit
+            extra = lax.dot_general(
+                beside[k].T, spread, (((1,), (0,)), ((), ())),
+                precision=lax.Precision.HIGHEST, preferred_element_type=jnp.float32,
+            )[0:unit]
+            scale = rate[r0 : r0 + unit, :]
+            for l in range(levels):
+                dest[l, r0 : r0 + unit, :] += scale * extra[:, l * LANES : (l + 1) * LANES]
+        for row, used, h in lines:
+            scale = rate[pl.ds(row, 1), :]
+            for l in range(levels):
+                more = jnp.where(used, scale * h[l : l + 1], 0.0)
+                dest[l, pl.ds(row, 1), :] = dest[l, pl.ds(row, 1), :] + more
+
+    def edge_columns(blocks_of):
+        made = []
+        for k in range(nu):
+            both = jnp.zeros((unit, LANES), jnp.float32)
+            for l in range(levels):
+                block = blocks_of(l, k)
+                first = block if l == 0 else pltpu.roll(block, l, 1)
+                both = jnp.where(lane == l, first, both)
+                both = jnp.where(lane == levels + l, pltpu.roll(block, levels + l + 1, 1), both)
+            turned = both.T[0:8]
+            if unit < LANES:
+                blank = jnp.zeros((8, LANES - unit), jnp.float32)
+                turned = jnp.concatenate([turned, blank], axis=1)
+            made.append(turned)
+        return made
+
+    def prepare_next(s, dest, found, columns):
+        beside, lines = found
+        pack, stage = packs[s], stages[s]
+        rank = lax.broadcasted_iota(jnp.int32, (8, LANES), 0)
+        ends = []
+        for row, used, h in lines:
+            twice = h + pltpu.roll(h, levels, 0)
+            at_end = small_lane == jnp.where(rank < levels, 0, LANES - 1)
+            ends.append(jnp.sum(jnp.where(at_end, twice, 0.0), axis=1, keepdims=True))
+        for k in range(nu):
+            total_add = beside[k]
+            for (row, used, _), end in zip(lines, ends):
+                at = jnp.where(used, row - k * unit, -1)
+                hit = small_lane == at
+                if unit < LANES:
+                    hit = jnp.logical_and(hit, small_lane < unit)
+                total_add = total_add + jnp.where(hit, end, 0.0)
+            fresh = columns[k] + rate_columns[k] * total_add
+            first, last = fresh[0:levels], fresh[levels : 2 * levels]
+            stage[2 + k] = first
+            stage[2 + nu + k] = last
+            pack[base + short + k] = jnp.where(left, first, last)
+        for n, (row, _, _) in enumerate(lines):
+            near_cells = jnp.zeros((8, LANES), jnp.float32)
             for k in range(nu):
-                x = field[l, k * unit : (k + 1) * unit, :]
-                j = k * 2 * levels + l
-                w = columns[0:unit, j : j + 1]
-                e = columns[0:unit, j + levels : j + levels + 1]
-                west_of = jnp.where(lane == 0, w, pltpu.roll(x, 1, 1))
-                east_of = jnp.where(lane == LANES - 1, e, pltpu.roll(x, LANES - 1, 1))
-                hsum[l, 8 + k * unit : 8 + (k + 1) * unit, :] = x + west_of + east_of
-        for l in range(levels):
-            for k in range(nu):
-                r0 = k * unit
-                x = field[l, r0 : r0 + unit, :]
-                upper = jnp.where(
-                    local_row == top_hit - r0, ghost_top[l : l + 1], hsum[l, 7 + r0 : 7 + r0 + unit, :]
-                )
-                lower = jnp.where(
-                    local_row == bottom_hit - r0,
-                    ghost_bottom[l : l + 1],
-                    hsum[l, 9 + r0 : 9 + r0 + unit, :],
-                )
-                box = upper + hsum[l, 8 + r0 : 8 + r0 + unit, :] + lower
-                dest[l, r0 : r0 + unit, :] = x + rate[r0 : r0 + unit, :] * (box - 9.0 * x)
+                near_cells = near_cells + jnp.where(small_lane == row - k * unit, beside[k], 0.0)
+            cells = jnp.sum(near_cells, axis=1, keepdims=True) + jnp.zeros((8, LANES), jnp.float32)
+            more = jnp.where(small_lane == 0, cells, 0.0) + jnp.where(
+                small_lane == LANES - 1, pltpu.roll(cells, 8 - levels, 0), 0.0
+            )
+            for other_row, used, h in lines:
+                more = more + jnp.where(jnp.logical_and(used, other_row == row), h, 0.0)
+            scale = rate[pl.ds(row, 1), :]
+            for l in range(levels):
+                line = dest[l, pl.ds(row, 1), :] + scale * more[l : l + 1]
+                if n < 2:
+                    stage[n, l : l + 1, :] = line
+                else:
+                    for k in range(nw):
+                        part = line if k == 0 else jnp.roll(line, -k * unit, axis=1)
+                        pack[base + (n - 2) * nw + k, l : l + 1, :] = part
 
     loads[0].wait()
-    prepare(0)
+    prepare(0, field)
     loads[1].wait()
     loads[2].wait()
     rate[...] = rate[...] * area[...] * 0.125
     pl.semaphore_wait(barrier, ndev - 1)
+    for l in range(levels):
+        hsum[l, 7:8, :] = jnp.zeros((1, LANES), jnp.float32)
+        hsum[l, 8 + rows : 9 + rows, :] = jnp.zeros((1, LANES), jnp.float32)
+    src, found = field, None
     for s in range(SWEEPS):
+        final = s == SWEEPS - 1
+        dest = out if final else (other if src is field else field)
         send(s)
+        if s == 0:
+            rate_columns = edge_columns(lambda l, k: rate[k * unit : (k + 1) * unit, :])
+        else:
+            complete(src, found)
+        partial(src, dest)
+        if not final:
+            columns = edge_columns(lambda l, k: dest[l, k * unit : (k + 1) * unit, :])
         receive(s)
-        sweep(s, out if s == SWEEPS - 1 else field)
-        if s < SWEEPS - 1:
-            prepare(s + 1)
+        found = gather(s)
+        if final:
+            complete(dest, found)
+        else:
+            prepare_next(s + 1, dest, found, columns)
+        src = dest
     for s in range(SWEEPS):
         finish(s)
 
@@ -328,16 +452,15 @@
     nu, nw = rows // unit, width // unit
     count = 2 * (nw + 2) + nu + 2
     picked_rows = -(-count * levels // 8) * 8
-    col_rows = -(-nu * 2 * levels // 8) * 8
     full = 2 * nw + nu
     scratch = [
+        pltpu.VMEM((levels, rows, width), jnp.float32),
         pltpu.VMEM((levels, rows, width), jnp.float32),
         pltpu.VMEM((rows, width), jnp.float32),
         pltpu.VMEM((rows, width), jnp.float32),
         pltpu.VMEM((levels, rows + 16, width), jnp.float32),
         pltpu.VMEM((picked_rows, LANES), jnp.float32),
         pltpu.VMEM((picked_rows, LANES), jnp.int32),
-        pltpu.VMEM((col_rows, LANES), jnp.float32),
     ]
     scratch += [pltpu.VMEM((nr * nc * full, levels, LANES), jnp.float32)] * SWEEPS
     scratch += [pltpu.VMEM((2 + 2 * nu, levels, LANES), jnp.float32)] * SWEEPS

time: 37.7 us -> 35.6 us (0.944)
  Pallas kernels: 31.9 us -> 29.8 us
    pallas_call x1, Pallas kernels: 31.9 us -> 29.8 us  [on_device(): pl.pallas_call(functools.partial(kernel, (levels, rows, width, nr, nc)),...]
where the time goes in v2:
time: 35.6 us; the launch traced here: 35.4 us
  Pallas kernels  29.8 us (84%)
  local copies, waits for them, and re-layouts  5.56 us (16%)
    pallas_call x1, Pallas kernels, on_device(): pl.pallas_call(functools.partial(kernel, (levels, rows, width, nr, nc)),...  29.8 us
    unnamed x13, local copies, waits for them, and re-layouts  5.56 us

profile of v2, /device:TPU:0, one launch (start us, length us, event | category | flops | bytes accessed | tf_op | source)
XLA Modules:
  0.0 35.4 jit_solution(2159804601470061415)
XLA Ops:
  0.0 0.0 copy-start
  0.0 1.0 %copy-done = f32[2,384,128]{2,1,0:T(8,128)S(1)} copy-done((f32[2,384,128]{2,1,0:T(8,128)S(1)}, f32[2,384,128]{2,1,0:T(8,128)}, u32[]{:S(2)}) %copy-start) | copy-done | bytes 393240
  1.0 0.0 copy-start.1
  1.0 0.9 %copy-done.1 = f32[384,128]{1,0:T(8,128)S(1)} copy-done((f32[384,128]{1,0:T(8,128)S(1)}, f32[384,128]{1,0:T(8,128)}, u32[]{:S(2)}) %copy-start.1) | copy-done | bytes 196632
  1.9 0.0 copy-start.2
  1.9 0.9 %copy-done.2 = f32[384,128]{1,0:T(8,128)S(1)} copy-done((f32[384,128]{1,0:T(8,128)S(1)}, f32[384,128]{1,0:T(8,128)}, u32[]{:S(2)}) %copy-start.2) | copy-done | bytes 196632
  2.9 0.0 copy-start.3
  2.9 0.7 %copy-done.3 = s32[24]{0:T(128)S(1)} copy-done((s32[24]{0:T(128)S(1)}, s32[24]{0:T(128)}, u32[]{:S(2)}) %copy-start.3) | copy-done | bytes 120
  3.5 0.0 copy-start.4
  3.5 0.7 %copy-done.4 = s32[24]{0:T(128)S(1)} copy-done((s32[24]{0:T(128)S(1)}, s32[24]{0:T(128)}, u32[]{:S(2)}) %copy-start.4) | copy-done | bytes 120
  4.2 0.0 copy-start.5
  4.2 0.7 %copy-done.5 = s32[24]{0:T(128)S(1)} copy-done((s32[24]{0:T(128)S(1)}, s32[24]{0:T(128)}, u32[]{:S(2)}) %copy-start.5) | copy-done | bytes 120
  4.8 29.8 %shard_map.64 = f32[2,384,128]{2,1,0:T(8,128)S(1)} custom-call(f32[2,384,128]{2,1,0:T(8,128)S(1)} %copy-done, f32[384,128]{1,0:T(8,128)S(1)} %copy-done.1, f32[384,128]{1,0:T(8,128)S(1)} %copy-done.2, s32[24]{0:T(128)S(1)} %copy-done.3, s32[24]{0:T(128)S(1)} %copy-done.4, s32[24]{0:T(128)S(1)} %copy-done.5), custom_call_target="tpu_custom_call" | custom-call | tf_op jit(solution)/shard_map/pallas_call | solution.py:472
  34.7 0.7 %copy.8 = f32[2,384,128]{2,1,0:T(8,128)} copy(f32[2,384,128]{2,1,0:T(8,128)S(1)} %shard_map.64) | data formatting | bytes 786432
Async XLA Ops:
  0.0 1.0 %copy-start = (f32[2,384,128]{2,1,0:T(8,128)S(1)}, f32[2,384,128]{2,1,0:T(8,128)}, u32[]{:S(2)}) copy-start(f32[2,384,128]{2,1,0:T(8,128)} %noise.1) | copy-start | bytes 1179652
  1.0 0.9 %copy-start.1 = (f32[384,128]{1,0:T(8,128)S(1)}, f32[384,128]{1,0:T(8,128)}, u32[]{:S(2)}) copy-start(f32[384,128]{1,0:T(8,128)} %kappa.1) | copy-start | bytes 589828
  1.9 0.9 %copy-start.2 = (f32[384,128]{1,0:T(8,128)S(1)}, f32[384,128]{1,0:T(8,128)}, u32[]{:S(2)}) copy-start(f32[384,128]{1,0:T(8,128)} %metric.1) | copy-start | bytes 589828
  2.9 0.7 %copy-start.3 = (s32[24]{0:T(128)S(1)}, s32[24]{0:T(128)}, u32[]{:S(2)}) copy-start(s32[24]{0:T(128)} %esrc_in.1) | copy-start | bytes 292
  3.5 0.7 %copy-start.4 = (s32[24]{0:T(128)S(1)}, s32[24]{0:T(128)}, u32[]{:S(2)}) copy-start(s32[24]{0:T(128)} %erev_in.1) | copy-start | bytes 292
  4.2 0.7 %copy-start.5 = (s32[24]{0:T(128)S(1)}, s32[24]{0:T(128)}, u32[]{:S(2)}) copy-start(s32[24]{0:T(128)} %csrc_in.1) | copy-start | bytes 292

commit v3 on v2

--- a/solution.py
+++ b/solution.py
@@ -28,7 +28,7 @@
     nu = rows // unit
     nw = width // unit
     per_face = face // unit
-    short, full = 2 * nw, 2 * nw + nu
+    full = 2 * nw + nu
 
     i = lax.axis_index("row")
     c = lax.axis_index("col")
@@ -75,15 +75,23 @@
     top_hit = jnp.where(has_top, top_row, -1)
     bottom_hit = jnp.where(has_bottom, bottom_row, -1)
 
+    def two_lines(row):
+        return lax.rem(row * rows + offset, face) + rows > face
+
+    both_lines = two_lines(i)
+    side_from = jnp.where(both_lines, 2 * nw, nw)
+
     def place(line, u):
         f = lax.div(line, 4)
         e = lax.rem(line, 4)
         row_stored = lax.rem(f * face + jnp.where(e == 1, face - 1, 0) + total - offset, total)
-        row_at = (lax.div(row_stored, rows) * nc + lax.div(u, nw)) * full + e * nw + lax.rem(u, nw)
+        owner = lax.div(row_stored, rows)
+        slot = jnp.where(two_lines(owner), e * nw, 0)
+        row_at = (owner * nc + lax.div(u, nw)) * full + slot + lax.rem(u, nw)
         side_stored = lax.rem(f * face + u * unit + total - offset, total)
         d = lax.div(side_stored, rows)
         k = lax.div(side_stored - d * rows, unit)
-        side_at = (d * nc + jnp.where(e == 3, nc - 1, 0)) * full + short + k
+        side_at = (d * nc + jnp.where(e == 3, nc - 1, 0)) * full + jnp.where(two_lines(d), 2 * nw, nw) + k
         return jnp.where(e < 2, row_at, side_at)
 
     def ghost_unit(edge, u):
@@ -136,16 +144,6 @@
         unit - 1 - lax.broadcasted_iota(jnp.int32, (picked.shape[0], LANES), 1) + LANES, LANES
     )
 
-    wide = (8, levels * LANES)
-    goal = lax.broadcasted_iota(jnp.int32, wide, 1)
-    source = lax.broadcasted_iota(jnp.int32, wide, 0)
-    spread = jnp.zeros(wide, jnp.float32)
-    for l in range(levels):
-        spread = jnp.where(jnp.logical_and(source == l, goal == l * LANES), 1.0, spread)
-        spread = jnp.where(
-            jnp.logical_and(source == levels + l, goal == (l + 1) * LANES - 1), 1.0, spread
-        )
-
     base = me * full
     up = lax.rem(i + nr - 1, nr)
     down = lax.rem(i + 1, nr)
@@ -157,7 +155,7 @@
         for l in range(levels):
             stage[0, l : l + 1, :] = field[l, 0:1, :]
             stage[1, l : l + 1, :] = field[l, rows - 1 : rows, :]
-            for e, row in ((0, top_at), (1, bottom_at)):
+            for e, row in ((0, jnp.where(has_top, top_at, bottom_at)), (1, bottom_at)):
                 line = field[l, pl.ds(row, 1), :]
                 for k in range(nw):
                     part = line if k == 0 else jnp.roll(line, -k * unit, axis=1)
@@ -173,7 +171,7 @@
                 first = turned[2 * l + 1 : 2 * l + 2, :]
                 stage[2 + k, l : l + 1, 0:unit] = first
                 stage[2 + nu + k, l : l + 1, 0:unit] = last
-                pack[base + short + k, l : l + 1, 0:unit] = jnp.where(left, first, last)
+                pack[base + side_from + k, l : l + 1, 0:unit] = jnp.where(left, first, last)
 
     def send(s):
         pack, stage, halo = packs[s], stages[s], halos[s]
@@ -205,40 +203,40 @@
         near(2, 6 + nu, nu, (i, west))
         near(2 + nu, 6, nu, (i, east))
 
-        @pl.when(side)
-        def _():
-            far(full)
-
-        @pl.when(jnp.logical_not(side))
-        def _():
-            far(short)
-
-    everything = 2 * nr * full + (nc - 2) * nr * short
-
-    def pack_wait(s, sem, side_units, mid_units):
+        for is_side in (True, False):
+            for has_two in (True, False):
+                size = (2 if has_two else 1) * nw + (nu if is_side else 0)
+                pl.when(jnp.logical_and(side == is_side, both_lines == has_two))(
+                    functools.partial(far, size)
+                )
+
+    doubles = sum((r * rows + offset) % face + rows > face for r in range(nr))
+    everything = nc * nw * (nr + doubles) + 2 * nr * nu
+
+    def pack_wait(s, sem, sending):
         pack = packs[s]
 
-        def take(units):
+        def take(size):
+            units = (ndev - 1) * size if sending else everything - size
             part = pack.at[pl.ds(0, units)]
             pltpu.make_async_copy(part, part, sem.at[s]).wait()
 
-        @pl.when(side)
-        def _():
-            take(side_units)
-
-        @pl.when(jnp.logical_not(side))
-        def _():
-            take(mid_units)
+        for is_side in (True, False):
+            for has_two in (True, False):
+                size = (2 if has_two else 1) * nw + (nu if is_side else 0)
+                pl.when(jnp.logical_and(side == is_side, both_lines == has_two))(
+                    functools.partial(take, size)
+                )
 
     def receive(s):
         halo = halos[s]
         pltpu.make_async_copy(halo, halo, halo_recv.at[s]).wait()
-        pack_wait(s, pack_recv, everything - full, everything - short)
+        pack_wait(s, pack_recv, False)
 
     def finish(s):
         halo = halos[s]
         pltpu.make_async_copy(halo, halo, halo_send.at[s]).wait()
-        pack_wait(s, pack_send, (ndev - 1) * full, (ndev - 1) * short)
+        pack_wait(s, pack_send, True)
 
     def triple(mid, before, after):
         mid, before, after = (
@@ -342,13 +340,15 @@
         beside, lines = found
         for k in range(nu):
             r0 = k * unit
-            extra = lax.dot_general(
-                beside[k].T, spread, (((1,), (0,)), ((), ())),
-                precision=lax.Precision.HIGHEST, preferred_element_type=jnp.float32,
-            )[0:unit]
+            turned = beside[k].T[0:unit]
             scale = rate[r0 : r0 + unit, :]
             for l in range(levels):
-                dest[l, r0 : r0 + unit, :] += scale * extra[:, l * LANES : (l + 1) * LANES]
+                extra = jnp.where(
+                    lane == 0,
+                    turned[:, l : l + 1],
+                    jnp.where(lane == LANES - 1, turned[:, levels + l : levels + l + 1], 0.0),
+                )
+                dest[l, r0 : r0 + unit, :] += scale * extra
         for row, used, h in lines:
             scale = rate[pl.ds(row, 1), :]
             for l in range(levels):
@@ -380,6 +380,26 @@
             twice = h + pltpu.roll(h, levels, 0)
             at_end = small_lane == jnp.where(rank < levels, 0, LANES - 1)
             ends.append(jnp.sum(jnp.where(at_end, twice, 0.0), axis=1, keepdims=True))
+        for n, (row, _, _) in enumerate(lines):
+            row = jnp.where(has_top, row, bottom_at) if n == 2 else row
+            near_cells = jnp.zeros((8, LANES), jnp.float32)
+            for k in range(nu):
+                near_cells = near_cells + jnp.where(small_lane == row - k * unit, beside[k], 0.0)
+            cells = jnp.sum(near_cells, axis=1, keepdims=True) + jnp.zeros((8, LANES), jnp.float32)
+            more = jnp.where(small_lane == 0, cells, 0.0) + jnp.where(
+                small_lane == LANES - 1, pltpu.roll(cells, 8 - levels, 0), 0.0
+            )
+            for other_row, used, h in lines:
+                more = more + jnp.where(jnp.logical_and(used, other_row == row), h, 0.0)
+            scale = rate[pl.ds(row, 1), :]
+            for l in range(levels):
+                line = dest[l, pl.ds(row, 1), :] + scale * more[l : l + 1]
+                if n < 2:
+                    stage[n, l : l + 1, :] = line
+                else:
+                    for k in range(nw):
+                        part = line if k == 0 else jnp.roll(line, -k * unit, axis=1)
+                        pack[base + (n - 2) * nw + k, l : l + 1, :] = part
         for k in range(nu):
             total_add = beside[k]
             for (row, used, _), end in zip(lines, ends):
@@ -392,26 +412,7 @@
             first, last = fresh[0:levels], fresh[levels : 2 * levels]
             stage[2 + k] = first
             stage[2 + nu + k] = last
-            pack[base + short + k] = jnp.where(left, first, last)
-        for n, (row, _, _) in enumerate(lines):
-            near_cells = jnp.zeros((8, LANES), jnp.float32)
-            for k in range(nu):
-                near_cells = near_cells + jnp.where(small_lane == row - k * unit, beside[k], 0.0)
-            cells = jnp.sum(near_cells, axis=1, keepdims=True) + jnp.zeros((8, LANES), jnp.float32)
-            more = jnp.where(small_lane == 0, cells, 0.0) + jnp.where(
-                small_lane == LANES - 1, pltpu.roll(cells, 8 - levels, 0), 0.0
-            )
-            for other_row, used, h in lines:
-                more = more + jnp.where(jnp.logical_and(used, other_row == row), h, 0.0)
-            scale = rate[pl.ds(row, 1), :]
-            for l in range(levels):
-                line = dest[l, pl.ds(row, 1), :] + scale * more[l : l + 1]
-                if n < 2:
-                    stage[n, l : l + 1, :] = line
-                else:
-                    for k in range(nw):
-                        part = line if k == 0 else jnp.roll(line, -k * unit, axis=1)
-                        pack[base + (n - 2) * nw + k, l : l + 1, :] = part
+            pack[base + side_from + k] = jnp.where(left, first, last)
 
     loads[0].wait()
     prepare(0, field)

time: 35.6 us -> 35.3 us (level)
  no operation moved by 1% of the time
where the time goes in v3:
time: 35.3 us; the launch traced here: 35.1 us
  Pallas kernels  29.5 us (84%)
  local copies, waits for them, and re-layouts  5.56 us (16%)
    pallas_call x1, Pallas kernels, on_device(): pl.pallas_call(functools.partial(kernel, (levels, rows, width, nr, nc)),...  29.5 us
    unnamed x13, local copies, waits for them, and re-layouts  5.56 us

profile of v3, /device:TPU:0, one launch (start us, length us, event | category | flops | bytes accessed | tf_op | source)
XLA Modules:
  0.0 35.1 jit_solution(6491673747419165077)
XLA Ops:
  0.0 0.0 copy-start
  0.0 1.0 %copy-done = f32[2,384,128]{2,1,0:T(8,128)S(1)} copy-done((f32[2,384,128]{2,1,0:T(8,128)S(1)}, f32[2,384,128]{2,1,0:T(8,128)}, u32[]{:S(2)}) %copy-start) | copy-done | bytes 393240
  1.0 0.0 copy-start.1
  1.0 0.9 %copy-done.1 = f32[384,128]{1,0:T(8,128)S(1)} copy-done((f32[384,128]{1,0:T(8,128)S(1)}, f32[384,128]{1,0:T(8,128)}, u32[]{:S(2)}) %copy-start.1) | copy-done | bytes 196632
  1.9 0.0 copy-start.2
  1.9 0.9 %copy-done.2 = f32[384,128]{1,0:T(8,128)S(1)} copy-done((f32[384,128]{1,0:T(8,128)S(1)}, f32[384,128]{1,0:T(8,128)}, u32[]{:S(2)}) %copy-start.2) | copy-done | bytes 196632
  2.9 0.0 copy-start.3
  2.9 0.7 %copy-done.3 = s32[24]{0:T(128)S(1)} copy-done((s32[24]{0:T(128)S(1)}, s32[24]{0:T(128)}, u32[]{:S(2)}) %copy-start.3) | copy-done | bytes 120
  3.5 0.0 copy-start.4
  3.5 0.7 %copy-done.4 = s32[24]{0:T(128)S(1)} copy-done((s32[24]{0:T(128)S(1)}, s32[24]{0:T(128)}, u32[]{:S(2)}) %copy-start.4) | copy-done | bytes 120
  4.2 0.0 copy-start.5
  4.2 0.7 %copy-done.5 = s32[24]{0:T(128)S(1)} copy-done((s32[24]{0:T(128)S(1)}, s32[24]{0:T(128)}, u32[]{:S(2)}) %copy-start.5) | copy-done | bytes 120
  4.8 29.5 %shard_map.64 = f32[2,384,128]{2,1,0:T(8,128)S(1)} custom-call(f32[2,384,128]{2,1,0:T(8,128)S(1)} %copy-done, f32[384,128]{1,0:T(8,128)S(1)} %copy-done.1, f32[384,128]{1,0:T(8,128)S(1)} %copy-done.2, s32[24]{0:T(128)S(1)} %copy-done.3, s32[24]{0:T(128)S(1)} %copy-done.4, s32[24]{0:T(128)S(1)} %copy-done.5), custom_call_target="tpu_custom_call" | custom-call | tf_op jit(solution)/shard_map/pallas_call | solution.py:473
  34.3 0.7 %copy.8 = f32[2,384,128]{2,1,0:T(8,128)} copy(f32[2,384,128]{2,1,0:T(8,128)S(1)} %shard_map.64) | data formatting | bytes 786432
Async XLA Ops:
  0.0 1.0 %copy-start = (f32[2,384,128]{2,1,0:T(8,128)S(1)}, f32[2,384,128]{2,1,0:T(8,128)}, u32[]{:S(2)}) copy-start(f32[2,384,128]{2,1,0:T(8,128)} %noise.1) | copy-start | bytes 1179652
  1.0 0.9 %copy-start.1 = (f32[384,128]{1,0:T(8,128)S(1)}, f32[384,128]{1,0:T(8,128)}, u32[]{:S(2)}) copy-start(f32[384,128]{1,0:T(8,128)} %kappa.1) | copy-start | bytes 589828
  1.9 0.9 %copy-start.2 = (f32[384,128]{1,0:T(8,128)S(1)}, f32[384,128]{1,0:T(8,128)}, u32[]{:S(2)}) copy-start(f32[384,128]{1,0:T(8,128)} %metric.1) | copy-start | bytes 589828
  2.9 0.7 %copy-start.3 = (s32[24]{0:T(128)S(1)}, s32[24]{0:T(128)}, u32[]{:S(2)}) copy-start(s32[24]{0:T(128)} %esrc_in.1) | copy-start | bytes 292
  3.5 0.7 %copy-start.4 = (s32[24]{0:T(128)S(1)}, s32[24]{0:T(128)}, u32[]{:S(2)}) copy-start(s32[24]{0:T(128)} %erev_in.1) | copy-start | bytes 292
  4.2 0.7 %copy-start.5 = (s32[24]{0:T(128)S(1)}, s32[24]{0:T(128)}, u32[]{:S(2)}) copy-start(s32[24]{0:T(128)} %csrc_in.1) | copy-start | bytes 292
